TPU v7x, 128 devices: a whole 4x4x4 slice. The times are simulated.
128 devices in a mesh: row: 16 (over x, z), col: 8 (over y, core).
Axes of the slice: x: 4, y: 4, z: 4, core: 2. Of those that a mesh axis runs over, the one named last changes fastest.
Arguments:
- root_inverse: float32 [2, 2048, 4, 1024], P(None, 'row', None, 'col'), as said below
- child_coupling: float32 [2, 2, 2048, 2, 1024], P(None, None, 'row', None, 'col'), may hold values from -0.046875 to 0.046875
- child_inverse: float32 [2, 1, 2048, 2, 1024], P(None, None, 'row', None, 'col'), as said below
- pattern: int32 [2, 32], replicated, may hold values 0 or 1
Outputs:
- sigma_root: float32 [2, 2048, 4, 1024], P(None, 'row', None, 'col')
- sigma_coupling: float32 [2, 2, 2048, 2, 1024], P(None, None, 'row', None, 'col')
- sigma_child: float32 [2, 128, 2, 1024], P(None, None, None, 'col')
Inputs may be any that keep to these rules, and one draw needn't show every extreme that they name: `root_inverse`: read row-major as a 4096 x 4096 matrix it is lower triangular with a positive diagonal. `child_inverse`: read row-major each child's 2048 x 2048 matrix is lower triangular with a positive diagonal. `pattern`: 1 where child j's separator couples to root supernode i, else 0.
All inputs are finite; a program needn't handle non-finite values.
Results may differ from a plain program's by a relative error of at most 0.00013.
Values sent between devices are 32-bit elements; how exact they have to be, the bound alone decides.
No kernel may reach another device: no remote copies, remote signals or barrier semaphores. Data moves between devices by JAX's collectives and lax.ppermute only.
A program may use at most 128 MiB of HBM per device.

v0:
```python
import jax
import jax.numpy as jnp
from jax import lax
from jax.sharding import PartitionSpec as P

B = 128
NR = 4096
NC = 2048


def spread(value, axis, source):
    kept = jnp.where(lax.axis_index(axis) == source, value, 0).astype(value.dtype)
    return lax.psum(kept, axis)


def local(root_inverse, child_coupling, child_inverse, pattern):
    highest = lax.Precision.HIGHEST
    rows_axis = lax.axis_size("row")
    cols_axis = lax.axis_size("col")
    my_row = lax.axis_index("row")
    root_blocks, width, col_blocks, _ = root_inverse.shape
    child_count = child_coupling.shape[0]
    child_columns = child_coupling.shape[3]
    local_rows = root_blocks * width
    block_ids = jnp.arange(root_blocks, dtype=jnp.int32) * rows_axis + my_row
    matches = (jnp.arange(NR // B, dtype=jnp.int32)[None, :] == block_ids[:, None]).astype(
        jnp.float32
    )
    keep = jnp.einsum("jn,an->ja", pattern.astype(jnp.float32), matches)
    coupled = child_coupling * keep[:, :, None, None, None]
    root_panel, child_panel = (
        lax.all_gather(root_inverse, "row", axis=1, tiled=True),
        lax.all_gather(child_inverse, "row", axis=2, tiled=True),
    )
    columns = root_panel.reshape(NR, col_blocks * width)
    groups = rows_axis // cols_axis
    chosen = lax.dynamic_index_in_dim(
        columns.reshape(NR, root_blocks, groups, width), my_row // cols_axis, 2, False
    )
    mirrored = spread(chosen.reshape(NR, local_rows), "col", my_row % cols_axis)
    sigma_local = jnp.einsum("km,kn->mn", mirrored, columns, precision=highest)
    sigma_root = sigma_local.reshape(root_blocks, width, col_blocks, width)
    sigma_rows, coupling_rows = (
        lax.all_gather(sigma_root, "col", axis=3, tiled=True),
        lax.all_gather(coupled, "col", axis=4, tiled=True),
    )
    coupling_panel = coupling_rows.reshape(child_count, local_rows, NC)
    inverse_columns = child_panel.reshape(child_count, NC, child_columns * width)
    update = jnp.einsum("jmk,jkn->jmn", coupling_panel, inverse_columns, precision=highest)
    sigma_split = sigma_rows.reshape(local_rows, root_blocks, rows_axis * width)
    update_split = update.reshape(child_count, root_blocks, width, child_columns * width)
    product = jnp.einsum(
        "mak,jakn->jmn",
        sigma_split,
        lax.all_gather(update_split, "row", axis=2, tiled=True),
        precision=highest,
    )
    coupling_sigma = -(
        product.reshape(child_count, root_blocks, width, child_columns * width)
        * keep[:, :, None, None]
    )
    local_inverse = child_inverse.reshape(child_count, -1, child_columns, width)
    first_part = jnp.einsum("jkcr,jkcs->jcrs", local_inverse, local_inverse, precision=highest)
    update_blocks = update.reshape(child_count, local_rows, child_columns, width)
    sigma_blocks = coupling_sigma.reshape(child_count, local_rows, child_columns, width)
    second_part = jnp.einsum("jkcr,jkcs->jcrs", update_blocks, sigma_blocks, precision=highest)
    summed = lax.psum(first_part - second_part, "row")
    sigma_child = summed.transpose(0, 2, 1, 3)
    return (
        sigma_root,
        coupling_sigma.reshape(child_count, root_blocks, width, child_columns, width),
        sigma_child,
    )


def solution(mesh):
    in_specs = (
        P(None, "row", None, "col"),
        P(None, None, "row", None, "col"),
        P(None, None, "row", None, "col"),
        P(),
    )
    out_specs = (
        P(None, "row", None, "col"),
        P(None, None, "row", None, "col"),
        P(None, None, None, "col"),
    )
    return jax.shard_map(local, mesh=mesh, in_specs=in_specs, out_specs=out_specs, check_vma=False)
```

profile of v0, /device:TPU:0, one launch (start us, length us, event | category | flops | bytes accessed | tf_op | source)
XLA Modules:
  0.0 490.8 jit_solution(11845554919135694700)
XLA Ops:
  7.2 0.0 all-gather.6.cloned.1.call-start
  7.2 0.7 all-gather.6.cloned.1.call-update
  7.9 0.0 all-reduce.3.cloned.1.call-start
  8.0 75.6 %all-gather.6.cloned.1.call-done = f32[2,2048,4,128]{3,2,1,0:T(4,128)} async-done(((f32[2,128,4,128]{3,2,1,0:T(4,128)}), f32[2,2048,4,128]{3,2,1,0:T(4,128)}) %all-gather.6.cloned.1.call-update) | async-done | bytes 8388624 | tf_op jit(solution)/shard_map/all_gather | solution.py:32
  83.6 7.3 %broadcast_select_fusion = f32[4096,2,1,128]{3,2,1,0:T(1,128)} fusion(pred[]{:T(512)S(6)} %eq.18, f32[4096,2,2,128]{3,2,1,0:T(2,128)} %bitcast.53, s32[]{:T(128)S(6)} %select_n.29), kind=kLoop, calls=%fused_computation.1 | loop fusion | flops 1048576 | bytes 8388613 | tf_op jit(solution)/shard_map/jit(_where)/select_n | solution.py:12
  90.8 10.2 %copy.19 = f32[4096,2,1,128]{0,3,1,2:T(8,128)} copy(f32[4096,2,1,128]{3,2,1,0:T(1,128)} %broadcast_select_fusion) | data formatting | bytes 8388608 | tf_op jit(solution)/shard_map/jit(_where)/select_n | solution.py:12
  101.0 0.0 copy-start.3
  101.0 0.0 copy-start.2
  101.0 0.0 all-reduce.3.cloned.1.call-update
  101.0 0.0 all-gather.8.cloned.1.call-start
  101.1 0.6 copy-done.3
  101.7 0.2 convolution_bitcast_fusion
  101.9 0.1 copy.21
  102.0 0.1 copy-done.2
  102.1 1.0 broadcast_multiply_fusion
  103.1 0.0 all-gather.8.cloned.1.call-update
  103.1 0.0 all-gather.10.cloned.1.call-start
  103.2 0.5 all-gather.10.cloned.1.call-update
  103.7 0.0 all-gather.14.cloned.1.call-start
  103.7 7.6 %copy.44 = f32[512,8,4,128]{3,1,2,0:T(8,128)} copy(f32[512,8,4,128]{3,2,1,0:T(4,128)} %bitcast.54) | data formatting | bytes 16777216
  111.3 9.0 %copy.20 = f32[4096,512]{0,1:T(8,128)} copy(f32[4096,512]{1,0:T(8,128)} %bitcast.52) | data formatting | bytes 16777216 | tf_op jit(solution)/shard_map/reshape | solution.py:35
  120.3 53.0 %all-reduce.3.cloned.1.call-done = f32[2,128,4096]{2,1,0:T(8,128)} async-done(((f32[2,128,4096]{2,1,0:T(8,128)}), f32[2,128,4096]{2,1,0:T(8,128)}) %all-reduce.3.cloned.1.call-update) | async-done | bytes 4194320 | tf_op jit(solution)/shard_map/psum | solution.py:13
  173.3 11.0 %fusion = f32[2,128,4,128]{3,1,2,0:T(8,128)} fusion(f32[4,128,4096,1]{2,1,0,3:T(8,128)} %bitcast.51, f32[2,128,4096]{2,1,0:T(8,128)} %all-reduce.3.cloned.1.call-done), kind=kOutput, calls=%fused_computation.2 | convolution fusion | flops 6442450944 | bytes 13107200 | tf_op jit(solution)/shard_map/km,kn->mn/dot_general | solution.py:41
  184.3 0.0 all-gather.14.cloned.1.call-update
  184.3 0.0 all-gather.12.cloned.1.call-start
  184.4 27.3 %all-gather.8.cloned.1.call-done = f32[2,2,128,2,1024]{4,3,2,1,0:T(2,128)} async-done(((f32[2,2,128,2,128]{4,3,2,1,0:T(2,128)}), f32[2,2,128,2,1024]{4,3,2,1,0:T(2,128)}) %all-gather.8.cloned.1.call-update) | async-done | bytes 4194320 | tf_op jit(solution)/shard_map/all_gather | solution.py:45
  211.7 6.6 %reshape.53 = f32[2,256,2048]{2,1,0:T(8,128)} reshape(f32[2,2,128,2,1024]{4,3,2,1,0:T(2,128)} %all-gather.8.cloned.1.call-done) | data formatting | bytes 8388608 | tf_op jit(solution)/shard_map/reshape | solution.py:47
  218.3 48.1 %all-gather.10.cloned.1.call-done = f32[2,1,2048,2,128]{4,3,2,1,0:T(2,128)} async-done(((f32[2,1,128,2,128]{4,3,2,1,0:T(2,128)}), f32[2,1,2048,2,128]{4,3,2,1,0:T(2,128)}) %all-gather.10.cloned.1.call-update) | async-done | bytes 4194320 | tf_op jit(solution)/shard_map/all_gather | solution.py:33
  266.4 6.4 %reshape.54 = f32[2,2048,256]{2,1,0:T(8,128)} reshape(f32[2,1,2048,2,128]{4,3,2,1,0:T(2,128)} %all-gather.10.cloned.1.call-done) | data formatting | bytes 8388608 | tf_op jit(solution)/shard_map/reshape | solution.py:48
  272.9 8.1 %fusion.14 = f32[2,256,256]{2,1,0:T(8,128)S(1)} fusion(f32[2,256,2048]{2,1,0:T(8,128)} %reshape.53, f32[2,2048,256]{2,1,0:T(8,128)} %reshape.54), kind=kOutput, calls=%fused_computation.23 | convolution fusion | flops 3221225472 | bytes 8912896 | tf_op jit(solution)/shard_map/jmk,jkn->jmn/dot_general | solution.py:49
  280.9 1.0 copy.22
  281.9 0.0 all-gather.12.cloned.1.call-update
  282.0 0.2 all-reduce.5.cloned.1.call-start
  282.2 0.1 broadcast_bitcast_fusion
  282.3 0.2 copy.37
  282.5 21.7 %all-gather.14.cloned.1.call-done = f32[2,128,4,1024]{3,1,2,0:T(8,128)} async-done(((f32[2,128,4,128]{3,1,2,0:T(8,128)}), f32[2,128,4,1024]{3,1,2,0:T(8,128)}) %all-gather.14.cloned.1.call-update) | async-done | bytes 4194320 | tf_op jit(solution)/shard_map/all_gather | solution.py:44
  304.2 7.3 %copy.23 = f32[2,128,4,1024]{1,0,3,2:T(2,128)} copy(f32[2,128,4,1024]{3,1,2,0:T(8,128)} %all-gather.14.cloned.1.call-done) | data formatting | bytes 8388608 | tf_op jit(solution)/shard_map/all_gather | solution.py:44
  311.5 6.4 %reshape.56 = f32[256,2,2048]{0,2,1:T(8,128)} reshape(f32[2,128,4,1024]{1,0,3,2:T(2,128)} %copy.23) | data formatting | bytes 8388608 | tf_op jit(solution)/shard_map/reshape | solution.py:50
  317.9 0.0 copy-start.1
  317.9 0.0 copy-start
  317.9 68.3 %all-gather.12.cloned.1.call-done = f32[2,2,2048,256]{2,3,1,0:T(8,128)} async-done(((f32[2,2,128,256]{2,3,1,0:T(8,128)}), f32[2,2,2048,256]{2,3,1,0:T(8,128)}) %all-gather.12.cloned.1.call-update) | async-done | bytes 8388624 | tf_op jit(solution)/shard_map/all_gather | solution.py:55
  386.2 9.8 %fusion.2 = f32[2,256,256,1]{2,1,3,0:T(8,128)S(1)} fusion(f32[2,2,2048,256]{2,3,1,0:T(8,128)} %all-gather.12.cloned.1.call-done, f32[256,2,2048]{0,2,1:T(8,128)} %reshape.56), kind=kOutput, calls=%fused_computation.4 | convolution fusion | flops 6442450944 | bytes 13107200 | tf_op jit(solution)/shard_map/mak,jakn->jmn/dot_general | solution.py:52
  396.0 0.2 copy.29
  396.2 0.8 fusion.5
  397.0 0.0 copy-done.1
  397.0 1.3 fusion.4
  398.3 0.0 all-reduce.5.cloned.1.call-update
  398.3 0.0 copy-done
  398.3 1.1 copy.31
  399.5 0.3 reshape.57
  399.7 0.4 copy.25
  400.2 1.1 multiply_negate_fusion
  401.2 80.9 %all-reduce.5.cloned.1.call-done = f32[2,128,2,128]{3,1,2,0:T(8,128)} async-done(((f32[2,128,2,128]{3,1,2,0:T(8,128)}), f32[2,128,2,128]{3,1,2,0:T(8,128)}) %all-reduce.5.cloned.1.call-update) | async-done | bytes 262160 | tf_op jit(solution)/shard_map/psum | solution.py:67
  482.1 1.9 copy.32
  (2 shorter events, 0.0 us)
Async XLA Ops:
  7.2 76.4 %all-gather.6.cloned.1.call-start = ((), (), s32[]{:S(2)}) async-start(), calls=%async_computation | async-start | bytes 8912896 | tf_op jit(solution)/shard_map/all_gather | solution.py:32
  7.9 165.4 %all-reduce.3.cloned.1.call-start = ((), (), s32[]{:S(2)}) async-start(), calls=%async_computation.1 | async-start | bytes 8388608 | tf_op jit(solution)/shard_map/psum | solution.py:13
  101.0 0.7 copy-start.3
  101.0 1.1 copy-start.2
  101.0 110.6 %all-gather.8.cloned.1.call-start = ((), (), s32[]{:S(2)}) async-start(), calls=%async_computation.2 | async-start | bytes 4718592 | tf_op jit(solution)/shard_map/all_gather | solution.py:45
  103.1 163.3 %all-gather.10.cloned.1.call-start = ((), (), s32[]{:S(2)}) async-start(), calls=%async_computation.3 | async-start | bytes 4456448 | tf_op jit(solution)/shard_map/all_gather | solution.py:33
  103.7 200.5 %all-gather.14.cloned.1.call-start = ((), (), s32[]{:S(2)}) async-start(), calls=%async_computation.5 | async-start | bytes 4718592 | tf_op jit(solution)/shard_map/all_gather | solution.py:44
  184.3 201.9 %all-gather.12.cloned.1.call-start = ((), (), s32[]{:S(2)}) async-start(), calls=%async_computation.4 | async-start | bytes 8912896 | tf_op jit(solution)/shard_map/all_gather | solution.py:55
  282.0 200.1 %all-reduce.5.cloned.1.call-start = ((), (), s32[]{:S(2)}) async-start(), calls=%async_computation.6 | async-start | bytes 524288 | tf_op jit(solution)/shard_map/psum | solution.py:67
  317.9 79.1 %copy-start.1 = (f32[2,1,128,2,128]{4,3,2,1,0:T(2,128)S(1)}, f32[2,1,128,2,128]{4,3,2,1,0:T(2,128)}, u32[]{:S(2)}) copy-start(f32[2,1,128,2,128]{4,3,2,1,0:T(2,128)} %param.6) | copy-start | bytes 786436
  317.9 80.4 %copy-start = (f32[2,128,4,128]{3,1,2,0:T(8,128)S(1)}, f32[2,128,4,128]{3,1,2,0:T(8,128)}, u32[]{:S(2)}) copy-start(f32[2,128,4,128]{3,1,2,0:T(8,128)} %fusion) | copy-start | bytes 1572868
Sparse Core Ops, SparseCore 0:
  10.2 73.3 all-gather.5
  101.1 72.0 all-reduce.2
  175.5 36.0 all-gather.7
  213.7 52.6 all-gather.9
  268.5 35.6 all-gather.13
  306.7 79.4 all-gather.11
  398.4 83.6 all-reduce.4
where the time goes:
time: 492 us; the launch traced here: 491 us
  waiting for transfers between devices  376 us (76%)
  local copies, waits for them, and re-layouts  59.4 us (12%)
  matrix products  31.1 us (6%)
  between operations  14.2 us (3%)
  other arithmetic  9.37 us (2%)
    psum x1, waiting for transfers between devices, local(): summed = lax.psum(first_part - second_part, 'row')  80.9 us
    all_gather x1, waiting for transfers between devices, local(): lax.all_gather(root_inverse, 'row', axis=1, tiled=True)  75.6 us
    all_gather x1, waiting for transfers between devices, local(): lax.all_gather(update_split, 'row', axis=2, tiled=True)  68.3 us
    psum x1, waiting for transfers between devices, spread(): return lax.psum(kept, axis)  53 us
    all_gather x1, waiting for transfers between devices, local(): lax.all_gather(child_inverse, 'row', axis=2, tiled=True)  48.1 us
    all_gather x1, waiting for transfers between devices, local(): lax.all_gather(coupled, 'col', axis=4, tiled=True)  27.3 us
    all_gather x1, waiting for transfers between devices, local(): lax.all_gather(sigma_root, 'col', axis=3, tiled=True)  21.7 us
    unnamed x13, local copies, waits for them, and re-layouts  11.4 us
  transfers between devices with their start and end apart: 7, of which 7 were waited for; matrix products, arithmetic and copies ran while one was open for 14% of the time, Pallas kernels for 0%

commit v1 on v0

--- a/solution.py
+++ b/solution.py
@@ -64,7 +64,7 @@
     update_blocks = update.reshape(child_count, local_rows, child_columns, width)
     sigma_blocks = coupling_sigma.reshape(child_count, local_rows, child_columns, width)
     second_part = jnp.einsum("jkcr,jkcs->jcrs", update_blocks, sigma_blocks, precision=highest)
-    summed = lax.psum(first_part - second_part, "row")
+    summed = jnp.sum(lax.all_gather(first_part - second_part, "row"), axis=0)
     sigma_child = summed.transpose(0, 2, 1, 3)
     return (
         sigma_root,

time: 492 us -> 461 us (0.937)
  waiting for transfers between devices: 376 us -> 343 us
    psum x1 -> x0, waiting for transfers between devices: 80.9 us -> none  [local(): summed = lax.psum(first_part - second_part, 'row')]
    all_gather x0 -> x1, waiting for transfers between devices: none -> 48.2 us  [local(): summed = jnp.sum(lax.all_gather(first_part - second_part, 'row'), axis=0)]
  transfers between devices with their start and end apart: 7 -> 7, of which waited for: 7 -> 7; matrix products, arithmetic and copies ran while one was open for 14% -> 15% of each run, Pallas kernels for 0% -> 0%
where the time goes in v1:
time: 461 us; the launch traced here: 460 us
  waiting for transfers between devices  343 us (74%)
  local copies, waits for them, and re-layouts  58.5 us (13%)
  matrix products  31.1 us (7%)
  between operations  14.2 us (3%)
  other arithmetic  11.8 us (3%)
    all_gather x1, waiting for transfers between devices, local(): lax.all_gather(root_inverse, 'row', axis=1, tiled=True)  75.6 us
    all_gather x1, waiting for transfers between devices, local(): lax.all_gather(update_split, 'row', axis=2, tiled=True)  68.3 us
    psum x1, waiting for transfers between devices, spread(): return lax.psum(kept, axis)  53 us
    all_gather x1, waiting for transfers between devices, local(): summed = jnp.sum(lax.all_gather(first_part - second_part, 'row'), axis=0)  48.2 us
    all_gather x1, waiting for transfers between devices, local(): lax.all_gather(child_inverse, 'row', axis=2, tiled=True)  48.1 us
    all_gather x1, waiting for transfers between devices, local(): lax.all_gather(coupled, 'col', axis=4, tiled=True)  27.3 us
    all_gather x1, waiting for transfers between devices, local(): lax.all_gather(sigma_root, 'col', axis=3, tiled=True)  21.7 us
    dot_general x1, matrix products, local(): sigma_local = jnp.einsum('km,kn->mn', mirrored, columns, precision=highest)  11 us
  transfers between devices with their start and end apart: 7, of which 7 were waited for; matrix products, arithmetic and copies ran while one was open for 15% of the time, Pallas kernels for 0%

profile of v1, /device:TPU:0, one launch (start us, length us, event | category | flops | bytes accessed | tf_op | source)
XLA Modules:
  0.0 459.6 jit_solution(628824909064304684)
XLA Ops:
  7.2 0.0 all-gather.8.cloned.1.call-start
  7.2 0.7 all-gather.8.cloned.1.call-update
  7.9 0.0 all-reduce.2.cloned.1.call-start
  8.0 75.6 %all-gather.8.cloned.1.call-done = f32[2,2048,4,128]{3,2,1,0:T(4,128)} async-done(((f32[2,128,4,128]{3,2,1,0:T(4,128)}), f32[2,2048,4,128]{3,2,1,0:T(4,128)}) %all-gather.8.cloned.1.call-update) | async-done | bytes 8388624 | tf_op jit(solution)/shard_map/all_gather | solution.py:32
  83.6 7.3 %broadcast_select_fusion = f32[4096,2,1,128]{3,2,1,0:T(1,128)} fusion(pred[]{:T(512)S(6)} %eq.18, f32[4096,2,2,128]{3,2,1,0:T(2,128)} %bitcast.53, s32[]{:T(128)S(6)} %select_n.29), kind=kLoop, calls=%fused_computation.1 | loop fusion | flops 1048576 | bytes 8388613 | tf_op jit(solution)/shard_map/jit(_where)/select_n | solution.py:12
  90.8 10.2 %copy.31 = f32[4096,2,1,128]{0,3,1,2:T(8,128)} copy(f32[4096,2,1,128]{3,2,1,0:T(1,128)} %broadcast_select_fusion) | data formatting | bytes 8388608 | tf_op jit(solution)/shard_map/jit(_where)/select_n | solution.py:12
  101.0 0.0 copy-start.3
  101.0 0.0 copy-start.2
  101.0 0.0 all-reduce.2.cloned.1.call-update
  101.0 0.0 all-gather.10.cloned.1.call-start
  101.1 0.6 copy-done.3
  101.7 0.2 convolution_bitcast_fusion
  101.9 0.1 copy.33
  102.0 0.1 copy-done.2
  102.1 1.0 broadcast_multiply_fusion
  103.1 0.0 all-gather.10.cloned.1.call-update
  103.1 0.0 all-gather.12.cloned.1.call-start
  103.2 0.5 all-gather.12.cloned.1.call-update
  103.7 0.0 all-gather.16.cloned.1.call-start
  103.7 7.6 %copy.56 = f32[512,8,4,128]{3,1,2,0:T(8,128)} copy(f32[512,8,4,128]{3,2,1,0:T(4,128)} %bitcast.54) | data formatting | bytes 16777216
  111.3 9.0 %copy.32 = f32[4096,512]{0,1:T(8,128)} copy(f32[4096,512]{1,0:T(8,128)} %bitcast.52) | data formatting | bytes 16777216 | tf_op jit(solution)/shard_map/reshape | solution.py:35
  120.3 53.0 %all-reduce.2.cloned.1.call-done = f32[2,128,4096]{2,1,0:T(8,128)} async-done(((f32[2,128,4096]{2,1,0:T(8,128)}), f32[2,128,4096]{2,1,0:T(8,128)}) %all-reduce.2.cloned.1.call-update) | async-done | bytes 4194320 | tf_op jit(solution)/shard_map/psum | solution.py:13
  173.3 11.0 %fusion = f32[2,128,4,128]{3,1,2,0:T(8,128)} fusion(f32[4,128,4096,1]{2,1,0,3:T(8,128)} %bitcast.51, f32[2,128,4096]{2,1,0:T(8,128)} %all-reduce.2.cloned.1.call-done), kind=kOutput, calls=%fused_computation.2 | convolution fusion | flops 6442450944 | bytes 13107200 | tf_op jit(solution)/shard_map/km,kn->mn/dot_general | solution.py:41
  184.3 0.0 all-gather.16.cloned.1.call-update
  184.3 0.0 all-gather.14.cloned.1.call-start
  184.4 27.3 %all-gather.10.cloned.1.call-done = f32[2,2,128,2,1024]{4,3,2,1,0:T(2,128)} async-done(((f32[2,2,128,2,128]{4,3,2,1,0:T(2,128)}), f32[2,2,128,2,1024]{4,3,2,1,0:T(2,128)}) %all-gather.10.cloned.1.call-update) | async-done | bytes 4194320 | tf_op jit(solution)/shard_map/all_gather | solution.py:45
  211.7 6.6 %reshape.53 = f32[2,256,2048]{2,1,0:T(8,128)} reshape(f32[2,2,128,2,1024]{4,3,2,1,0:T(2,128)} %all-gather.10.cloned.1.call-done) | data formatting | bytes 8388608 | tf_op jit(solution)/shard_map/reshape | solution.py:47
  218.3 48.1 %all-gather.12.cloned.1.call-done = f32[2,1,2048,2,128]{4,3,2,1,0:T(2,128)} async-done(((f32[2,1,128,2,128]{4,3,2,1,0:T(2,128)}), f32[2,1,2048,2,128]{4,3,2,1,0:T(2,128)}) %all-gather.12.cloned.1.call-update) | async-done | bytes 4194320 | tf_op jit(solution)/shard_map/all_gather | solution.py:33
  266.4 6.4 %reshape.54 = f32[2,2048,256]{2,1,0:T(8,128)} reshape(f32[2,1,2048,2,128]{4,3,2,1,0:T(2,128)} %all-gather.12.cloned.1.call-done) | data formatting | bytes 8388608 | tf_op jit(solution)/shard_map/reshape | solution.py:48
  272.9 8.1 %fusion.13 = f32[2,256,256]{2,1,0:T(8,128)S(1)} fusion(f32[2,256,2048]{2,1,0:T(8,128)} %reshape.53, f32[2,2048,256]{2,1,0:T(8,128)} %reshape.54), kind=kOutput, calls=%fused_computation.22 | convolution fusion | flops 3221225472 | bytes 8912896 | tf_op jit(solution)/shard_map/jmk,jkn->jmn/dot_general | solution.py:49
  280.9 1.0 copy.34
  281.9 0.0 all-gather.14.cloned.1.call-update
  282.0 0.2 all-gather.18.cloned.1.call-start
  282.2 0.1 broadcast_bitcast_fusion
  282.3 0.2 copy.49
  282.5 21.7 %all-gather.16.cloned.1.call-done = f32[2,128,4,1024]{3,1,2,0:T(8,128)} async-done(((f32[2,128,4,128]{3,1,2,0:T(8,128)}), f32[2,128,4,1024]{3,1,2,0:T(8,128)}) %all-gather.16.cloned.1.call-update) | async-done | bytes 4194320 | tf_op jit(solution)/shard_map/all_gather | solution.py:44
  304.2 7.3 %copy.35 = f32[2,128,4,1024]{1,0,3,2:T(2,128)} copy(f32[2,128,4,1024]{3,1,2,0:T(8,128)} %all-gather.16.cloned.1.call-done) | data formatting | bytes 8388608 | tf_op jit(solution)/shard_map/all_gather | solution.py:44
  311.5 6.4 %reshape.56 = f32[256,2,2048]{0,2,1:T(8,128)} reshape(f32[2,128,4,1024]{1,0,3,2:T(2,128)} %copy.35) | data formatting | bytes 8388608 | tf_op jit(solution)/shard_map/reshape | solution.py:50
  317.9 0.0 copy-start.1
  317.9 0.0 copy-start
  317.9 68.3 %all-gather.14.cloned.1.call-done = f32[2,2,2048,256]{2,3,1,0:T(8,128)} async-done(((f32[2,2,128,256]{2,3,1,0:T(8,128)}), f32[2,2,2048,256]{2,3,1,0:T(8,128)}) %all-gather.14.cloned.1.call-update) | async-done | bytes 8388624 | tf_op jit(solution)/shard_map/all_gather | solution.py:55
  386.2 9.8 %fusion.2 = f32[2,256,256,1]{2,1,3,0:T(8,128)S(1)} fusion(f32[2,2,2048,256]{2,3,1,0:T(8,128)} %all-gather.14.cloned.1.call-done, f32[256,2,2048]{0,2,1:T(8,128)} %reshape.56), kind=kOutput, calls=%fused_computation.4 | convolution fusion | flops 6442450944 | bytes 13107200 | tf_op jit(solution)/shard_map/mak,jakn->jmn/dot_general | solution.py:52
  396.0 0.2 copy.41
  396.2 0.8 fusion.4
  397.0 0.0 copy-done.1
  397.0 1.3 convolution_subtract_fusion
  398.3 0.0 all-gather.18.cloned.1.call-update
  398.3 0.0 copy-done
  398.3 1.1 copy.43
  399.5 0.3 reshape.57
  399.7 0.4 copy.37
  400.2 1.1 multiply_negate_fusion
  401.2 48.2 %all-gather.18.cloned.1.call-done = f32[32,2,128,128]{3,2,1,0:T(8,128)} async-done(((f32[2,2,128,128]{3,2,1,0:T(8,128)}), f32[32,2,128,128]{3,2,1,0:T(8,128)}) %all-gather.18.cloned.1.call-update) | async-done | bytes 4194320 | tf_op jit(solution)/shard_map/all_gather | solution.py:67
  449.4 2.4 reduce_sum.9
  451.8 0.9 copy.44
  (2 shorter events, 0.0 us)
Async XLA Ops:
  7.2 76.4 %all-gather.8.cloned.1.call-start = ((), (), s32[]{:S(2)}) async-start(), calls=%async_computation | async-start | bytes 8912896 | tf_op jit(solution)/shard_map/all_gather | solution.py:32
  7.9 165.4 %all-reduce.2.cloned.1.call-start = ((), (), s32[]{:S(2)}) async-start(), calls=%async_computation.1 | async-start | bytes 8388608 | tf_op jit(solution)/shard_map/psum | solution.py:13
  101.0 0.7 copy-start.3
  101.0 1.1 copy-start.2
  101.0 110.6 %all-gather.10.cloned.1.call-start = ((), (), s32[]{:S(2)}) async-start(), calls=%async_computation.2 | async-start | bytes 4718592 | tf_op jit(solution)/shard_map/all_gather | solution.py:45
  103.1 163.3 %all-gather.12.cloned.1.call-start = ((), (), s32[]{:S(2)}) async-start(), calls=%async_computation.3 | async-start | bytes 4456448 | tf_op jit(solution)/shard_map/all_gather | solution.py:33
  103.7 200.5 %all-gather.16.cloned.1.call-start = ((), (), s32[]{:S(2)}) async-start(), calls=%async_computation.5 | async-start | bytes 4718592 | tf_op jit(solution)/shard_map/all_gather | solution.py:44
  184.3 201.9 %all-gather.14.cloned.1.call-start = ((), (), s32[]{:S(2)}) async-start(), calls=%async_computation.4 | async-start | bytes 8912896 | tf_op jit(solution)/shard_map/all_gather | solution.py:55
  282.0 167.5 %all-gather.18.cloned.1.call-start = ((), (), s32[]{:S(2)}) async-start(), calls=%async_computation.6 | async-start | bytes 4456448 | tf_op jit(solution)/shard_map/all_gather | solution.py:67
  317.9 79.1 %copy-start.1 = (f32[2,1,128,2,128]{4,3,2,1,0:T(2,128)S(1)}, f32[2,1,128,2,128]{4,3,2,1,0:T(2,128)}, u32[]{:S(2)}) copy-start(f32[2,1,128,2,128]{4,3,2,1,0:T(2,128)} %param.6) | copy-start | bytes 786436
  317.9 80.4 %copy-start = (f32[2,128,4,128]{3,1,2,0:T(8,128)S(1)}, f32[2,128,4,128]{3,1,2,0:T(8,128)}, u32[]{:S(2)}) copy-start(f32[2,128,4,128]{3,1,2,0:T(8,128)} %fusion) | copy-start | bytes 1572868
Sparse Core Ops, SparseCore 0:
  10.2 73.3 all-gather.7
  101.1 72.0 all-reduce.1
  175.5 36.0 all-gather.9
  213.7 52.6 all-gather.11
  268.5 35.6 all-gather.15
  306.7 79.4 all-gather.13
  398.4 50.9 all-gather.17
